TPU v7x, 32 devices: a whole 2x2x4 slice. The times are simulated.
32 devices in a mesh: dp: 8 (over z, core), tensor: 4 (over y, x).
Axes of the slice: x: 2, y: 2, z: 4, core: 2. Of those that a mesh axis runs over, the one named last changes fastest.
Arguments:
- inputs: float32 [8192, 1024], P(('dp', 'tensor')), may hold values from -6 to 6
- teacher: float32 [8192, 1024], P(('dp', 'tensor')), may hold values from -6 to 6
- valid_mask: int32 [8, 1024], P('dp'), may hold values from 0 to 1, as said below
- documents: int32 [8, 1024], P('dp'), may hold values from 0 to 3, never falling along the last dimension, each value on 1 to 512 neighbouring positions
- picture_starts: int32 [8, 2], P('dp'), may hold values from 0 to 768, as said below
- w_query: bfloat16 [1024, 1024], P('dp', 'tensor'), may hold values from -0.25 to 0.25
- w_key: bfloat16 [1024, 1024], P('dp', 'tensor'), may hold values from -0.25 to 0.25
- w_value: bfloat16 [1024, 1024], P('dp', 'tensor'), may hold values from -0.1875 to 0.1875
- w_out: bfloat16 [1024, 1024], P('tensor', 'dp'), may hold values from -0.75 to 0.75
- w_gate: bfloat16 [1024, 2816], P('dp', 'tensor'), may hold values from -0.1875 to 0.1875
- w_up: bfloat16 [1024, 2816], P('dp', 'tensor'), may hold values from -0.1875 to 0.1875
- w_down: bfloat16 [2816, 1024], P('tensor', 'dp'), may hold values from -0.109375 to 0.109375
Outputs:
- output: float32 [8192, 1024], P(('dp', 'tensor'))
- loss_value: float32 [], replicated
- grad_inputs: float32 [8192, 1024], P(('dp', 'tensor'))
- grad_query: float32 [1024, 1024], P('dp', 'tensor')
- grad_key: float32 [1024, 1024], P('dp', 'tensor')
- grad_value: float32 [1024, 1024], P('dp', 'tensor')
- grad_out: float32 [1024, 1024], P('tensor', 'dp')
- grad_gate: float32 [1024, 2816], P('dp', 'tensor')
- grad_up: float32 [1024, 2816], P('dp', 'tensor')
- grad_down: float32 [2816, 1024], P('tensor', 'dp')
Inputs may be any that keep to these rules, and one draw needn't show every extreme that they name: `valid_mask`: position 0 of every sequence is valid. `documents`: ids never fall along a sequence; each document has 1 to 512 tokens. `picture_starts`: piece p of a sequence starts between p * 512 and p * 512 + 1024 / 2 - 256, so the pieces of a sequence never intersect.
All inputs are finite; a program needn't handle non-finite values.
Results may differ from a plain program's by a relative error of at most 0.017.
Values may be sent and summed in bfloat16 or wider, within the bound.
A program may use at most 128 MiB of HBM per device.

v0:
```python
import jax
import jax.numpy as jnp
from jax import lax
from jax.sharding import PartitionSpec as P

D = 1024
HD = 64
PIECE = 256


norm_eps = 1e-05
masked_score = -1e30


def layer_norm(values):
    centred = values - jnp.mean(values, axis=-1, keepdims=True)
    inv_std = lax.rsqrt(jnp.mean(centred * centred, axis=-1, keepdims=True) + norm_eps)
    return (centred * inv_std, inv_std)


def norm_back(normed, inv_std, grad_normed):
    mean_grad = jnp.mean(grad_normed, axis=-1, keepdims=True)
    mean_cross = jnp.mean(grad_normed * normed, axis=-1, keepdims=True)
    return inv_std * (grad_normed - mean_grad - normed * mean_cross)


def rotary_tables(length, head_width):
    half_width = head_width // 2
    frequency = 10000.0 ** (-2.0 * jnp.arange(half_width, dtype=jnp.float32) / head_width)
    angles = jnp.arange(length, dtype=jnp.float32)[:, None] * frequency[None, :]
    cosine = jnp.cos(angles)
    sine_part = jnp.sin(angles)
    return (
        jnp.concatenate([cosine, cosine], axis=1),
        jnp.concatenate([sine_part, sine_part], axis=1),
    )


def rotate(values, cosine, sine_part, seq_count, head_count):
    length, head_width = cosine.shape
    shaped = values.reshape(seq_count, length, head_count, head_width)
    half_width = head_width // 2
    turned = jnp.concatenate([-shaped[..., half_width:], shaped[..., :half_width]], axis=-1)
    result = shaped * cosine[None, :, None, :] + turned * sine_part[None, :, None, :]
    return result.reshape(values.shape)


def rotate_back(grads_in, cosine, sine_part, seq_count, head_count):
    length, head_width = cosine.shape
    shaped = grads_in.reshape(seq_count, length, head_count, head_width)
    half_width = head_width // 2
    scaled = shaped * sine_part[None, :, None, :]
    turned = jnp.concatenate([scaled[..., half_width:], -scaled[..., :half_width]], axis=-1)
    result = shaped * cosine[None, :, None, :] + turned
    return result.reshape(grads_in.shape)


def picture_ids(starts, length):
    positions = jnp.arange(length, dtype=jnp.int32)[None, :, None]
    inside = (positions >= starts[:, None, :]) & (positions < starts[:, None, :] + PIECE)
    labels = jnp.arange(1, starts.shape[1] + 1, dtype=jnp.int32)[None, None, :]
    return jnp.sum(jnp.where(inside, labels, 0), axis=2)


def allowed_block(doc_row, pic_row, valid_row, first_query, block_rows):
    query_pos = first_query + jnp.arange(block_rows, dtype=jnp.int32)
    key_pos = jnp.arange(doc_row.shape[0], dtype=jnp.int32)
    doc_query = lax.dynamic_slice_in_dim(doc_row, first_query, block_rows)
    pic_query = lax.dynamic_slice_in_dim(pic_row, first_query, block_rows)
    same_doc = doc_query[:, None] == doc_row[None, :]
    before = key_pos[None, :] <= query_pos[:, None]
    same_pic = (pic_query[:, None] == pic_row[None, :]) & (pic_query[:, None] > 0)
    itself = key_pos[None, :] == query_pos[:, None]
    usable = (valid_row[None, :] == 1) | itself
    return same_doc & (before | same_pic) & usable


def block_scores(queries, keys_rot, mask_parts, block_index, head_count, block_rows):
    documents, pictures, valid_mask = mask_parts
    length = documents.shape[1]
    per_seq = length // block_rows
    head_width = queries.shape[1] // head_count
    seq_id = block_index // per_seq
    first_query = block_index % per_seq * block_rows
    query_blk = lax.dynamic_slice_in_dim(queries, block_index * block_rows, block_rows, 0).reshape(
        block_rows, head_count, head_width
    )
    key_seq = keys_rot.reshape(length, head_count, head_width)
    scores = jnp.einsum(
        "qhd,khd->hqk", query_blk, key_seq, preferred_element_type=jnp.float32
    ) * head_width ** (-0.5)
    doc_row = lax.dynamic_index_in_dim(documents, seq_id, 0, keepdims=False)
    pic_row = lax.dynamic_index_in_dim(pictures, seq_id, 0, keepdims=False)
    valid_row = lax.dynamic_index_in_dim(valid_mask, seq_id, 0, keepdims=False)
    allowed = allowed_block(doc_row, pic_row, valid_row, first_query, block_rows)
    return (jnp.where(allowed[None], scores, masked_score), query_blk, key_seq, seq_id)


def attend_forward(queries, keys_rot, values, mask_parts, head_count):
    length = mask_parts[0].shape[1]
    block_rows = min(512, length)
    block_total = queries.shape[0] // block_rows
    head_width = queries.shape[1] // head_count

    def one_block(block_index):
        masked, query_blk, key_seq, seq_id = block_scores(
            queries, keys_rot, mask_parts, block_index, head_count, block_rows
        )
        value_seq = values.reshape(length, head_count, head_width)
        row_max = jnp.max(masked, axis=2, keepdims=True)
        exponent = jnp.exp(masked - row_max)
        row_sum = jnp.sum(exponent, axis=2, keepdims=True)
        probs_low = (exponent / row_sum).astype(jnp.bfloat16)
        mixed_blk = jnp.einsum(
            "hqk,khd->qhd", probs_low, value_seq, preferred_element_type=jnp.float32
        )
        log_sums = (row_max + jnp.log(row_sum))[..., 0]
        return (
            mixed_blk.astype(jnp.bfloat16).reshape(block_rows, head_count * head_width),
            log_sums,
        )

    mixed, log_sums = lax.map(one_block, jnp.arange(block_total, dtype=jnp.int32))
    return (mixed.reshape(queries.shape), log_sums)


def attend_backward(queries, keys_rot, values, grad_mixed, log_sums, mask_parts, head_count):
    length = mask_parts[0].shape[1]
    block_rows = min(512, length)
    block_total = queries.shape[0] // block_rows
    head_width = queries.shape[1] // head_count
    scale = head_width ** (-0.5)

    def one_block(running, pieces):
        grad_keys, grad_values = running
        block_index, sums_blk = pieces
        masked, query_blk, key_seq, seq_id = block_scores(
            queries, keys_rot, mask_parts, block_index, head_count, block_rows
        )
        value_seq = values.reshape(length, head_count, head_width)
        grad_blk = lax.dynamic_slice_in_dim(
            grad_mixed, block_index * block_rows, block_rows, 0
        ).reshape(block_rows, head_count, head_width)
        attn_probs = jnp.exp(masked - sums_blk[:, :, None])
        probs_low = attn_probs.astype(jnp.bfloat16)
        grad_probs = jnp.einsum(
            "qhd,khd->hqk", grad_blk, value_seq, preferred_element_type=jnp.float32
        )
        row_dots = jnp.sum(attn_probs * grad_probs, axis=2, keepdims=True)
        grad_scores = (attn_probs * (grad_probs - row_dots)).astype(jnp.bfloat16)
        query_part = (
            jnp.einsum("hqk,khd->qhd", grad_scores, key_seq, preferred_element_type=jnp.float32)
            * scale
        )
        key_part = (
            jnp.einsum("hqk,qhd->khd", grad_scores, query_blk, preferred_element_type=jnp.float32)
            * scale
        )
        value_part = jnp.einsum(
            "hqk,qhd->khd", probs_low, grad_blk, preferred_element_type=jnp.float32
        )
        first_key = seq_id * length
        key_now = grad_keys + key_part.reshape(length, head_count * head_width)
        value_now = grad_values + value_part.reshape(length, head_count * head_width)
        grad_keys = key_now
        grad_values = value_now
        return ((grad_keys, grad_values), query_part.reshape(block_rows, head_count * head_width))

    zero_rows = jnp.zeros(keys_rot.shape, jnp.float32)
    final_parts, grad_queries = lax.scan(
        one_block, (zero_rows, zero_rows), (jnp.arange(block_total, dtype=jnp.int32), log_sums)
    )
    return (grad_queries.reshape(queries.shape), final_parts[0], final_parts[1])


def gather_rows(block):
    return lax.all_gather(block, "tensor", axis=0, tiled=True)


def scatter_rows(partial_value):
    return lax.psum_scatter(partial_value, "tensor", scatter_dimension=0, tiled=True)


def per_device(
    inputs,
    teacher,
    valid_mask,
    documents,
    picture_starts,
    w_query,
    w_key,
    w_value,
    w_out,
    w_gate,
    w_up,
    w_down,
):
    tok_rows = inputs.shape[0]
    seq_count, length = valid_mask.shape
    head_count = w_query.shape[1] // HD
    tensor_rank = lax.axis_index("tensor")
    pictures = picture_ids(picture_starts, length)
    mask_parts = (documents, pictures, valid_mask)
    row_valid = lax.dynamic_slice_in_dim(
        valid_mask.reshape(-1), tensor_rank * tok_rows, tok_rows, 0
    ).astype(jnp.float32)[:, None]
    local_count = jnp.sum(row_valid)
    valid_total = lax.psum(local_count, ("dp", "tensor"))
    cosine, sine_part = rotary_tables(length, HD)
    normed_one, inv_one = layer_norm(inputs)
    rows_one = gather_rows(normed_one.astype(jnp.bfloat16))
    query_full, key_full, value_full, out_full = (
        lax.all_gather(w_query, "dp", axis=0, tiled=True),
        lax.all_gather(w_key, "dp", axis=0, tiled=True),
        lax.all_gather(w_value, "dp", axis=0, tiled=True),
        lax.all_gather(w_out, "dp", axis=1, tiled=True),
    )
    query_pre = jnp.dot(rows_one, query_full, preferred_element_type=jnp.float32)
    key_pre = jnp.dot(rows_one, key_full, preferred_element_type=jnp.float32)
    queries = rotate(query_pre, cosine, sine_part, seq_count, head_count).astype(jnp.bfloat16)
    keys_rot = rotate(key_pre, cosine, sine_part, seq_count, head_count).astype(jnp.bfloat16)
    values = jnp.dot(rows_one, value_full, preferred_element_type=jnp.float32).astype(jnp.bfloat16)
    mixed, log_sums = attend_forward(queries, keys_rot, values, mask_parts, head_count)
    middle = inputs + scatter_rows(jnp.dot(mixed, out_full, preferred_element_type=jnp.float32))
    normed_two, inv_two = layer_norm(middle)
    rows_two = gather_rows(normed_two.astype(jnp.bfloat16))
    gate_full, up_full, down_full = (
        lax.all_gather(w_gate, "dp", axis=0, tiled=True),
        lax.all_gather(w_up, "dp", axis=0, tiled=True),
        lax.all_gather(w_down, "dp", axis=1, tiled=True),
    )
    gate_pre = jnp.dot(rows_two, gate_full, preferred_element_type=jnp.float32)
    up_proj = jnp.dot(rows_two, up_full, preferred_element_type=jnp.float32)
    sigmoid_gate = jax.nn.sigmoid(gate_pre)
    hidden = (gate_pre * sigmoid_gate * up_proj).astype(jnp.bfloat16)
    output = middle + scatter_rows(jnp.dot(hidden, down_full, preferred_element_type=jnp.float32))
    deviation = output - teacher
    local_error = jnp.sum(row_valid * deviation * deviation)
    error_total = lax.psum(local_error, ("dp", "tensor"))
    loss_value = error_total / (D * valid_total)
    total_tokens = seq_count * length * lax.axis_size("dp")
    cotangent = row_valid * deviation * (total_tokens / valid_total)
    back_gate, back_up, back_down = (
        lax.all_gather(w_gate, "dp", axis=0, tiled=True),
        lax.all_gather(w_up, "dp", axis=0, tiled=True),
        lax.all_gather(w_down, "dp", axis=1, tiled=True),
    )
    grad_rows_mlp = gather_rows(cotangent.astype(jnp.bfloat16))
    down_term = jnp.einsum("gf,gd->fd", hidden, grad_rows_mlp, preferred_element_type=jnp.float32)
    grad_hidden = jnp.einsum(
        "gd,fd->gf", grad_rows_mlp, back_down, preferred_element_type=jnp.float32
    )
    grad_gate_low = (
        grad_hidden * up_proj * sigmoid_gate * (1.0 + gate_pre * (1.0 - sigmoid_gate))
    ).astype(jnp.bfloat16)
    grad_up_low = (grad_hidden * gate_pre * sigmoid_gate).astype(jnp.bfloat16)
    gate_term = jnp.einsum("gd,gf->df", rows_two, grad_gate_low, preferred_element_type=jnp.float32)
    up_term = jnp.einsum("gd,gf->df", rows_two, grad_up_low, preferred_element_type=jnp.float32)
    grad_rows_two = jnp.einsum(
        "gf,df->gd", grad_gate_low, back_gate, preferred_element_type=jnp.float32
    )
    grad_rows_two = grad_rows_two + jnp.einsum(
        "gf,df->gd", grad_up_low, back_up, preferred_element_type=jnp.float32
    )
    grad_gate, grad_up, grad_down = (
        lax.psum_scatter(
            gate_term.astype(jnp.bfloat16), "dp", scatter_dimension=0, tiled=True
        ).astype(jnp.float32),
        lax.psum_scatter(
            up_term.astype(jnp.bfloat16), "dp", scatter_dimension=0, tiled=True
        ).astype(jnp.float32),
        lax.psum_scatter(
            down_term.astype(jnp.bfloat16), "dp", scatter_dimension=1, tiled=True
        ).astype(jnp.float32),
    )
    grad_middle = cotangent + norm_back(normed_two, inv_two, scatter_rows(grad_rows_two))
    back_query, back_key, back_value, back_out = (
        lax.all_gather(w_query, "dp", axis=0, tiled=True),
        lax.all_gather(w_key, "dp", axis=0, tiled=True),
        lax.all_gather(w_value, "dp", axis=0, tiled=True),
        lax.all_gather(w_out, "dp", axis=1, tiled=True),
    )
    grad_rows_attn = gather_rows(grad_middle.astype(jnp.bfloat16))
    out_term = jnp.einsum("gc,gd->cd", mixed, grad_rows_attn, preferred_element_type=jnp.float32)
    grad_mixed = jnp.einsum(
        "gd,cd->gc", grad_rows_attn, back_out, preferred_element_type=jnp.float32
    ).astype(jnp.bfloat16)
    grad_queries, grad_keys, grad_values = attend_backward(
        queries, keys_rot, values, grad_mixed, log_sums, mask_parts, head_count
    )
    grad_query_low = rotate_back(grad_queries, cosine, sine_part, seq_count, head_count).astype(
        jnp.bfloat16
    )
    grad_key_low = rotate_back(grad_keys, cosine, sine_part, seq_count, head_count).astype(
        jnp.bfloat16
    )
    grad_value_low = grad_values.astype(jnp.bfloat16)
    query_term = jnp.einsum(
        "gd,gc->dc", rows_one, grad_query_low, preferred_element_type=jnp.float32
    )
    key_term = jnp.einsum("gd,gc->dc", rows_one, grad_key_low, preferred_element_type=jnp.float32)
    value_term = jnp.einsum(
        "gd,gc->dc", rows_one, grad_value_low, preferred_element_type=jnp.float32
    )
    grad_rows_one = jnp.einsum(
        "gc,dc->gd", grad_query_low, back_query, preferred_element_type=jnp.float32
    )
    grad_rows_one = grad_rows_one + jnp.einsum(
        "gc,dc->gd", grad_key_low, back_key, preferred_element_type=jnp.float32
    )
    grad_rows_one = grad_rows_one + jnp.einsum(
        "gc,dc->gd", grad_value_low, back_value, preferred_element_type=jnp.float32
    )
    grad_query, grad_key, grad_value, grad_out = (
        lax.psum_scatter(
            query_term.astype(jnp.bfloat16), "dp", scatter_dimension=0, tiled=True
        ).astype(jnp.float32),
        lax.psum_scatter(
            key_term.astype(jnp.bfloat16), "dp", scatter_dimension=0, tiled=True
        ).astype(jnp.float32),
        lax.psum_scatter(
            value_term.astype(jnp.bfloat16), "dp", scatter_dimension=0, tiled=True
        ).astype(jnp.float32),
        lax.psum_scatter(
            out_term.astype(jnp.bfloat16), "dp", scatter_dimension=1, tiled=True
        ).astype(jnp.float32),
    )
    grad_inputs = grad_middle + norm_back(normed_one, inv_one, scatter_rows(grad_rows_one))
    return (
        output,
        loss_value,
        grad_inputs,
        grad_query,
        grad_key,
        grad_value,
        grad_out,
        grad_gate,
        grad_up,
        grad_down,
    )


def solution(mesh):
    in_specs = (
        P(("dp", "tensor"), None),
        P(("dp", "tensor"), None),
        P("dp", None),
        P("dp", None),
        P("dp", None),
        P("dp", "tensor"),
        P("dp", "tensor"),
        P("dp", "tensor"),
        P("tensor", "dp"),
        P("dp", "tensor"),
        P("dp", "tensor"),
        P("tensor", "dp"),
    )
    out_specs = (
        P(("dp", "tensor"), None),
        P(),
        P(("dp", "tensor"), None),
        P("dp", "tensor"),
        P("dp", "tensor"),
        P("dp", "tensor"),
        P("tensor", "dp"),
        P("dp", "tensor"),
        P("dp", "tensor"),
        P("tensor", "dp"),
    )
    return jax.shard_map(
        per_device, mesh=mesh, in_specs=in_specs, out_specs=out_specs, check_vma=False
    )
```

profile of v0, /device:TPU:0, one launch (start us, length us, event | category | flops | bytes accessed | tf_op | source)
XLA Modules:
  0.0 800.5 jit_solution(4885230315111675707)
XLA Ops:
  14.7 16.6 %all_gather.41 = bf16[1024,256]{1,0:T(8,128)(2,1)S(1)} all-gather(bf16[128,256]{1,0:T(8,128)(2,1)S(1)} %copy-done.22), channel_id=1, replica_groups=mesh['dp'=8,'tensor'=4] {'dp'}, dimensions={0}, use_global_device_ids=true | all-gather | bytes 589824 | tf_op jit(solution)/shard_map/all_gather | solution.py:213
  31.3 14.7 %all_gather.42 = bf16[1024,256]{1,0:T(8,128)(2,1)S(1)} all-gather(bf16[128,256]{1,0:T(8,128)(2,1)S(1)} %copy-done.23), channel_id=1, replica_groups=mesh['dp'=8,'tensor'=4] {'dp'}, dimensions={0}, use_global_device_ids=true | all-gather | bytes 589824 | tf_op jit(solution)/shard_map/all_gather | solution.py:214
  46.0 16.2 %all_gather.43 = bf16[1024,256]{1,0:T(8,128)(2,1)} all-gather(bf16[128,256]{1,0:T(8,128)(2,1)S(1)} %copy-done.24), channel_id=1, replica_groups=mesh['dp'=8,'tensor'=4] {'dp'}, dimensions={0}, use_global_device_ids=true | all-gather | bytes 589824 | tf_op jit(solution)/shard_map/all_gather | solution.py:215
  62.3 15.0 %all_gather.44 = bf16[256,1024]{1,0:T(8,128)(2,1)} all-gather(bf16[256,128]{1,0:T(8,128)(2,1)S(1)} %copy-done.25), channel_id=1, replica_groups=mesh['dp'=8,'tensor'=4] {'dp'}, dimensions={1}, use_global_device_ids=true | all-gather | bytes 589824 | tf_op jit(solution)/shard_map/all_gather | solution.py:216
  86.3 25.2 %while.31 = (s32[]{:T(128)}, bf16[2,512,256]{2,1,0:T(8,128)(2,1)S(1)}, f32[2,4,512]{2,1,0:T(4,128)S(1)}, s32[2]{0:T(128)S(1)}, s32[1,1024]{1,0:T(1,128)S(1)}, /*...) while((s32[]{:T(128)}, ...), condition=%wide.region_6.7_spmd, body=%wide.region_3.6_spmd.sunk | while | flops 566886400 | bytes 30508412 | solution.py:123
  114.8 51.9 %reduce-scatter.20.cloned.1.call-done = f32[256,1024]{1,0:T(8,128)} async-done(((f32[1024,1024]{1,0:T(8,128)}), f32[256,1024]{1,0:T(8,128)}) %reduce-scatter.20.cloned.1.call-update) | async-done | bytes 1048592 | tf_op jit(solution)/shard_map/reduce_scatter | solution.py:181
  171.2 33.4 %all-gather.10.cloned.1.call-done = bf16[1024,1024]{1,0:T(8,128)(2,1)} async-done(((bf16[256,1024]{1,0:T(8,128)(2,1)}), bf16[1024,1024]{1,0:T(8,128)(2,1)}) %all-gather.10.cloned.1.call-update) | async-done | bytes 2097168 | tf_op jit(solution)/shard_map/all_gather | solution.py:177
  209.9 22.5 %all-gather.14.cloned.1.call-done = bf16[1024,704]{0,1:T(8,128)(2,1)} async-done(((bf16[128,704]{0,1:T(8,128)(2,1)}), bf16[1024,704]{0,1:T(8,128)(2,1)}) %all-gather.14.cloned.1.call-update) | async-done | bytes 1441808 | tf_op jit(solution)/shard_map/all_gather | solution.py:229
  232.4 6.8 multiply_convert_fusion.3
  239.2 20.0 %all-gather.16.cloned.1.call-done = bf16[704,1024]{1,0:T(8,128)(2,1)} async-done(((bf16[704,128]{1,0:T(8,128)(2,1)}), bf16[704,1024]{1,0:T(8,128)(2,1)}) %all-gather.16.cloned.1.call-update) | async-done | bytes 1441808 | tf_op jit(solution)/shard_map/all_gather | solution.py:230
  265.5 50.9 %reduce-scatter.22.cloned.1.call-done = f32[256,1024]{1,0:T(8,128)} async-done(((f32[1024,1024]{1,0:T(8,128)}), f32[256,1024]{1,0:T(8,128)}) %reduce-scatter.22.cloned.1.call-update) | async-done | bytes 1048592 | tf_op jit(solution)/shard_map/reduce_scatter | solution.py:181
  319.4 39.6 %all-reduce = (f32[]{:T(128)}, f32[]{:T(128)}) all-reduce(f32[]{:T(128)} %get-tuple-element.496, f32[]{:T(128)} %get-tuple-element.494), channel_id=1, replica_groups=mesh['dp'=8,'tensor'=4] {'dp','tensor'}, use_global_device_ids=true, to_apply=%region_12.13 | all-reduce | flops 2 | bytes 16 | tf_op jit(solution)/shard_map/psum | solution.py:239
  362.0 36.3 %all-gather.18.cloned.1.call-done = bf16[1024,1024]{1,0:T(8,128)(2,1)} async-done(((bf16[256,1024]{1,0:T(8,128)(2,1)}), bf16[1024,1024]{1,0:T(8,128)(2,1)}) %all-gather.18.cloned.1.call-update) | async-done | bytes 2097168 | tf_op jit(solution)/shard_map/all_gather | solution.py:177
  411.0 52.6 %reduce-scatter.24.cloned.1.call-done = f32[256,1024]{1,0:T(8,128)} async-done(((f32[1024,1024]{1,0:T(8,128)}), f32[256,1024]{1,0:T(8,128)}) %reduce-scatter.24.cloned.1.call-update) | async-done | bytes 1048592 | tf_op jit(solution)/shard_map/reduce_scatter | solution.py:181
  484.8 18.8 %all-gather.20.cloned.1.call-done = bf16[1024,1024]{1,0:T(8,128)(2,1)} async-done(((bf16[256,1024]{1,0:T(8,128)(2,1)}), bf16[1024,1024]{1,0:T(8,128)(2,1)}) %all-gather.20.cloned.1.call-update) | async-done | bytes 2097168 | tf_op jit(solution)/shard_map/all_gather | solution.py:177
  512.1 61.8 %while.32 = (s32[]{:T(128)}, f32[1024,256]{0,1:T(8,128)S(1)}, f32[1024,256]{0,1:T(8,128)S(1)}, f32[2,512,256]{1,0,2:T(2,128)}, s32[2]{0:T(128)S(1)}, /*index=5*/...) while((s32[]{:T(128)}, f32[1024,256]{0,1:T(8,128)S(1)}, ...), condition=%wide.region_20.21_spmd.clone, body=%wide.region_18.20_spmd.clone.sunk | while | flops 1379794944 | bytes 80307624 | solution.py:170
  532.6 10.3 %dynamic_update_slice.29 = f32[2,512,256]{1,0,2:T(2,128)} dynamic-update-slice(f32[2,512,256]{1,0,2:T(2,128)} %get-tuple-element.754, f32[1,512,256]{1,0,2:T(1,128)S(1)} %copy.73, s32[]{:T(128)S(6)} %copy.90, s32[]{:T(128)} %constant.195.clone.1..sunk.1, s32[]{:T(128)} %constant.195.clone.1..sunk.1) | dynamic-update-slice | bytes 1048580 | tf_op jit(solution)/shard_map/while/body/jit(dynamic_update_index_in_dim)/dynamic_update_slice | solution.py:170
  563.4 10.3 %dynamic_update_slice.29 = f32[2,512,256]{1,0,2:T(2,128)} dynamic-update-slice(f32[2,512,256]{1,0,2:T(2,128)} %get-tuple-element.754, f32[1,512,256]{1,0,2:T(1,128)S(1)} %copy.73, s32[]{:T(128)S(6)} %copy.90, s32[]{:T(128)} %constant.195.clone.1..sunk.1, s32[]{:T(128)} %constant.195.clone.1..sunk.1) | dynamic-update-slice | bytes 1048580 | tf_op jit(solution)/shard_map/while/body/jit(dynamic_update_index_in_dim)/dynamic_update_slice | solution.py:170
  602.1 6.6 reduce-scatter.36.cloned.1.call-done
  610.6 29.7 %reduce-scatter.34.cloned.1.call-done = bf16[128,256]{1,0:T(8,128)(2,1)} async-done(((bf16[1024,256]{1,0:T(8,128)(2,1)}), bf16[128,256]{1,0:T(8,128)(2,1)}) %reduce-scatter.34.cloned.1.call-update) | async-done | bytes 65552
  641.8 29.6 %reduce-scatter.32.cloned.1.call-done = bf16[128,256]{1,0:T(8,128)(2,1)} async-done(((bf16[1024,256]{1,0:T(8,128)(2,1)}), bf16[128,256]{1,0:T(8,128)(2,1)}) %reduce-scatter.32.cloned.1.call-update) | async-done | bytes 65552 | tf_op jit(solution)/shard_map/reduce_scatter | solution.py:321
  672.9 29.8 %reduce-scatter.30.cloned.1.call-done = bf16[128,256]{1,0:T(8,128)(2,1)} async-done(((bf16[1024,256]{1,0:T(8,128)(2,1)}), bf16[128,256]{1,0:T(8,128)(2,1)}) %reduce-scatter.30.cloned.1.call-update) | async-done | bytes 65552 | tf_op jit(solution)/shard_map/reduce_scatter | solution.py:318
  704.2 29.6 %reduce-scatter.28.cloned.1.call-done = bf16[128,256]{1,0:T(8,128)(2,1)} async-done(((bf16[1024,256]{1,0:T(8,128)(2,1)}), bf16[128,256]{1,0:T(8,128)(2,1)}) %reduce-scatter.28.cloned.1.call-update) | async-done | bytes 65552 | tf_op jit(solution)/shard_map/reduce_scatter | solution.py:315
  735.3 52.4 %reduce-scatter.26.cloned.1.call-done = f32[256,1024]{1,0:T(8,128)} async-done(((f32[1024,1024]{1,0:T(8,128)}), f32[256,1024]{1,0:T(8,128)}) %reduce-scatter.26.cloned.1.call-update) | async-done | bytes 1048592 | tf_op jit(solution)/shard_map/reduce_scatter | solution.py:181
  (256 shorter events, 176.3 us)
Async XLA Ops:
  8.0 69.2 %all-gather.8.cloned.1.call-start = ((), (), s32[]{:S(2)}) async-start(), calls=%async_computation.11 | async-start | bytes 2621440 | tf_op jit(solution)/shard_map/all_gather | solution.py:177
  9.5 52.8 %copy-start.25 = (bf16[256,128]{1,0:T(8,128)(2,1)S(1)}, bf16[256,128]{1,0:T(8,128)(2,1)}, u32[]{:S(2)}) copy-start(bf16[256,128]{1,0:T(8,128)(2,1)} %param.24) | copy-start | bytes 196612
  13.2 153.5 %reduce-scatter.20.cloned.1.call-start = ((), (), s32[]{:S(2)}) async-start(), calls=%async_computation.12 | async-start | bytes 5242880 | tf_op jit(solution)/shard_map/reduce_scatter | solution.py:181
  14.7 69.8 %copy-start.13 = (f32[1024,64]{0,1:T(8,128)}, f32[1024,64]{0,1:T(8,128)S(1)}, u32[]{:S(2)}) copy-start(f32[1024,64]{0,1:T(8,128)S(1)} %get-tuple-element.531) | copy-start | bytes 786436
  114.1 57.1 %all-gather.12.cloned.1.call-start = ((), (), s32[]{:S(2)}) async-start(), calls=%async_computation.14 | async-start | bytes 1622016 | tf_op jit(solution)/shard_map/all_gather | solution.py:228
  114.7 89.9 %all-gather.10.cloned.1.call-start = ((), (), s32[]{:S(2)}) async-start(), calls=%async_computation.13 | async-start | bytes 2621440 | tf_op jit(solution)/shard_map/all_gather | solution.py:177
  169.4 63.0 %all-gather.14.cloned.1.call-start = ((), (), s32[]{:S(2)}) async-start(), calls=%async_computation.15 | async-start | bytes 1622016 | tf_op jit(solution)/shard_map/all_gather | solution.py:229
  170.0 89.2 %all-gather.16.cloned.1.call-start = ((), (), s32[]{:S(2)}) async-start(), calls=%async_computation.16 | async-start | bytes 1622016 | tf_op jit(solution)/shard_map/all_gather | solution.py:230
  170.7 145.6 %reduce-scatter.22.cloned.1.call-start = ((), (), s32[]{:S(2)}) async-start(), calls=%async_computation.17 | async-start | bytes 5242880 | tf_op jit(solution)/shard_map/reduce_scatter | solution.py:181
  264.8 133.5 %all-gather.18.cloned.1.call-start = ((), (), s32[]{:S(2)}) async-start(), calls=%async_computation.18 | async-start | bytes 2621440 | tf_op jit(solution)/shard_map/all_gather | solution.py:177
  361.9 101.7 %reduce-scatter.24.cloned.1.call-start = ((), (), s32[]{:S(2)}) async-start(), calls=%async_computation.19 | async-start | bytes 5242880 | tf_op jit(solution)/shard_map/reduce_scatter | solution.py:181
  410.8 92.8 %all-gather.20.cloned.1.call-start = ((), (), s32[]{:S(2)}) async-start(), calls=%async_computation.20 | async-start | bytes 2621440 | tf_op jit(solution)/shard_map/all_gather | solution.py:177
  468.4 129.9 %reduce-scatter.40.cloned.1.call-start = ((), (), s32[]{:S(2)}) async-start(), calls=%async_computation.28 | async-start | bytes 1769472
  473.8 126.5 %reduce-scatter.38.cloned.1.call-start = ((), (), s32[]{:S(2)}) async-start(), calls=%async_computation.27 | async-start | bytes 1769472
  479.3 129.4 %reduce-scatter.36.cloned.1.call-start = ((), (), s32[]{:S(2)}) async-start(), calls=%async_computation.26 | async-start | bytes 1769472
  484.8 155.5 %reduce-scatter.34.cloned.1.call-start = ((), (), s32[]{:S(2)}) async-start(), calls=%async_computation.25 | async-start | bytes 589824
  508.8 162.6 %reduce-scatter.32.cloned.1.call-start = ((), (), s32[]{:S(2)}) async-start(), calls=%async_computation.24 | async-start | bytes 589824 | tf_op jit(solution)/shard_map/reduce_scatter | solution.py:321
  582.9 119.9 %reduce-scatter.30.cloned.1.call-start = ((), (), s32[]{:S(2)}) async-start(), calls=%async_computation.23 | async-start | bytes 589824 | tf_op jit(solution)/shard_map/reduce_scatter | solution.py:318
  588.7 145.2 %reduce-scatter.28.cloned.1.call-start = ((), (), s32[]{:S(2)}) async-start(), calls=%async_computation.22 | async-start | bytes 589824 | tf_op jit(solution)/shard_map/reduce_scatter | solution.py:315
  592.0 195.7 %reduce-scatter.26.cloned.1.call-start = ((), (), s32[]{:S(2)}) async-start(), calls=%async_computation.21 | async-start | bytes 5242880 | tf_op jit(solution)/shard_map/reduce_scatter | solution.py:181
  596.8 190.9 %copy-start.1 = (f32[256,1024]{1,0:T(8,128)S(1)}, f32[256,1024]{1,0:T(8,128)}, u32[]{:S(2)}) copy-start(f32[256,1024]{1,0:T(8,128)} %param.16) | copy-start | bytes 3145732
  596.8 190.9 %copy-start.27 = (f32[256]{0:T(256)S(1)}, f32[256]{0:T(256)}, u32[]{:S(2)}) copy-start(f32[256]{0:T(256)} %copy-done.26) | copy-start | bytes 3076
  596.9 190.9 %copy-start.29 = (f32[256]{0:T(256)S(1)}, f32[256]{0:T(256)}, u32[]{:S(2)}) copy-start(f32[256]{0:T(256)} %copy-done.28) | copy-start | bytes 3076
  598.3 191.0 %copy-start.10 = (f32[256,1024]{1,0:T(8,128)S(1)}, f32[256,1024]{1,0:T(8,128)}, u32[]{:S(2)}) copy-start(f32[256,1024]{1,0:T(8,128)} %get-tuple-element.493) | copy-start | bytes 3145732
  (29 other events, 339.6 us)
Sparse Core Ops, SparseCore 0:
  13.4 38.0 all-gather.7
  114.3 52.4 reduce-scatter.19
  362.1 36.1 all-gather.17
  410.9 52.6 reduce-scatter.23
Sparse Core Ops, SparseCore 1:
  116.3 26.1 all-gather.11
  169.5 35.1 all-gather.9
  206.2 26.2 all-gather.13
  234.1 25.0 all-gather.15
  264.9 51.4 reduce-scatter.21
  468.5 35.1 all-gather.19
  505.9 33.8 reduce-scatter.39
  542.0 31.9 reduce-scatter.37
  576.3 32.3 reduce-scatter.35
  611.1 29.1 reduce-scatter.33
  642.3 29.0 reduce-scatter.31
  673.8 28.9 reduce-scatter.29
  704.9 28.9 reduce-scatter.27
  737.1 50.6 reduce-scatter.25
where the time goes:
time: 807 us; the launch traced here: 801 us
  waiting for transfers between devices  466 us (58%)
  blocking collectives  102 us (13%)
  matrix products  98.1 us (12%)
  other arithmetic  51.6 us (6%)
  local copies, waits for them, and re-layouts  50.6 us (6%)
  between operations  19.7 us (2%)
  loops' own time  11 us (1%)
    reduce_scatter x4, waiting for transfers between devices, scatter_rows(): lax.psum_scatter(partial_value, 'tensor', scatter_dimension=0, tiled=True)  208 us
    all_gather x4, waiting for transfers between devices, gather_rows(): return lax.all_gather(block, 'tensor', axis=0, tiled=True)  88.5 us
    psum x1, blocking collectives, per_device(): error_total = lax.psum(local_error, ('dp', 'tensor'))  39.6 us
    unnamed x22, waiting for transfers between devices  38.2 us
    reduce_scatter x1, waiting for transfers between devices, per_device(): lax.psum_scatter(key_term.astype(jnp.bfloat16), 'dp', scatter_dimension=0...  29.8 us
    reduce_scatter x1, waiting for transfers between devices, per_device(): lax.psum_scatter(query_term.astype(jnp.bfloat16), 'dp', scatter_dimension...  29.6 us
    reduce_scatter x1, waiting for transfers between devices, per_device(): lax.psum_scatter(value_term.astype(jnp.bfloat16), 'dp', scatter_dimension...  29.6 us
    all_gather x1, waiting for transfers between devices, per_device(): lax.all_gather(w_up, 'dp', axis=0, tiled=True)  22.5 us
  transfers between devices with their start and end apart: 18, of which 14 were waited for; matrix products, arithmetic and copies ran while one was open for 16% of the time, Pallas kernels for 0%

commit v1 on v0

v1 whole, which is shorter than its diff:
```python
import functools

import jax
import jax.numpy as jnp
import numpy as np
from jax import lax
from jax.experimental import pallas as pl
from jax.experimental.pallas import tpu as pltpu
from jax.sharding import PartitionSpec as P

MESH = pl.DeviceIdType.MESH
HD = 64
PIECE = 256
EPS = 1e-5
MASKED = -1e30
BF = jnp.bfloat16
F32 = jnp.float32
NT = (((1,), (1,)), ((), ()))
NN = (((1,), (0,)), ((), ()))


def dot(a, b, dims=NN):
    return lax.dot_general(a, b, dims, preferred_element_type=F32)


def eye(n):
    return (
        lax.broadcasted_iota(jnp.int32, (n, n), 0) == lax.broadcasted_iota(jnp.int32, (n, n), 1)
    ).astype(F32).astype(BF)


def turned(a):
    return dot(eye(a.shape[1]), a, NT).astype(BF)


def mean_of(v):
    return jnp.sum(v, axis=1, keepdims=True) * (1.0 / v.shape[1])


def normed(v):
    centred = v - mean_of(v)
    inv = lax.rsqrt(mean_of(centred * centred) + EPS)
    return centred * inv, inv


def normed_back(n, inv, g):
    return inv * (g - mean_of(g) - n * mean_of(g * n))


class Geo:
    def __init__(self, n_dp, n_t, tok_rows, d_model, cols, hid):
        self.n_dp, self.n_t, self.R, self.D, self.c, self.f = n_dp, n_t, tok_rows, d_model, cols, hid
        self.C = n_dp // 2
        self.S = tok_rows * n_t
        self.H = cols // HD
        self.Dn = d_model // n_dp
        self.square = n_t == 4

    def place(self):
        self.d = lax.axis_index("dp")
        self.t = lax.axis_index("tensor")
        self.chip = self.d // 2
        self.core = self.d % 2
        if self.square:
            self.tx = self.t + 1 - 2 * (self.t % 2)
            self.ty = (self.t + 2) % 4
            self.td = 3 - self.t
            self.to = [self.tx, self.ty]
            self.arrive = [self.t, self.tx, self.ty, self.td]
            self.leave = [self.td, self.tx, self.ty, self.t]
        else:
            n = self.n_t
            self.to = [(self.t + k) % n for k in range(1, n)]
            self.arrive = [(self.t + n - k) % n for k in range(n)]
            self.leave = [(self.t + k) % n for k in range(1, n)] + [self.t]
        self.sib = self.d + 1 - 2 * self.core
        return self

    def zto(self, k):
        return ((self.chip + k) % self.C) * 2 + self.core

    def zfrom(self, k):
        return ((self.chip + self.C - k) % self.C) * 2 + self.core

    def rows(self, blk, first=0, count=None):
        count = self.R if count is None else count
        return pl.ds(pl.multiple_of(blk * self.R + first, count), count)

    def wrows(self, d):
        return pl.ds(pl.multiple_of(d * self.Dn, self.Dn), self.Dn)

    def greet(self, tensor=True, dp=True):
        bar = pltpu.get_barrier_semaphore()
        out = [(self.d, p) for p in self.to] if tensor else []
        if dp:
            out += [(self.zto(k), self.t) for k in range(1, self.C)] + [(self.sib, self.t)]
        for dev in out:
            pl.semaphore_signal(bar, inc=1, device_id=dev, device_id_type=MESH)
        pl.semaphore_wait(bar, len(out))


class Comm:
    def __init__(self, send_sem, recv_sem, me):
        self.ss, self.rs, self.me = send_sem, recv_sem, me
        self.n = 0
        self.pending = []

    def slots(self, k):
        self.n += k
        return list(range(self.n - k, self.n))

    def _copy(self, slot, src, dst, dev):
        return pltpu.make_async_remote_copy(
            src_ref=src, dst_ref=dst, send_sem=self.ss.at[slot], recv_sem=self.rs.at[slot],
            device_id=dev, device_id_type=MESH,
        )

    def send(self, slot, src, dst, dev):
        copy = self._copy(slot, src, dst, dev)
        copy.start()
        self.pending.append(copy)

    def recv(self, slot, dst, dev):
        self._copy(slot, dst, dst, dev).wait_recv()

    def finish(self):
        for copy in self.pending:
            copy.wait_send()
        self.pending = []


class Gather:
    def __init__(self, geo, comm, buf):
        self.g, self.comm, self.buf = geo, comm, buf
        g = geo
        if g.square:
            self.sx, self.sy = comm.slots(3), comm.slots(3)
            h0, h1 = self.half(g.t, 0), self.half(g.t, 1)
            comm.send(self.sx[0], h0, h0, (g.d, g.tx))
            comm.send(self.sy[1], h1, h1, (g.d, g.ty))
            comm.send(self.sx[1], h1, h1, (g.d, g.tx))
            comm.send(self.sy[0], h0, h0, (g.d, g.ty))
        else:
            self.s = comm.slots(g.n_t - 1)
            own = buf.at[g.rows(g.t)]
            for k, peer in enumerate(g.to):
                comm.send(self.s[k], own, own, (g.d, peer))

    def half(self, blk, i):
        h = self.g.R // 2
        return self.buf.at[self.g.rows(blk, i * h, h)]

    def relay(self):
        g, comm = self.g, self.comm
        if g.square:
            a = self.half(g.tx, 0)
            comm.recv(self.sx[0], a, (g.d, g.tx))
            comm.send(self.sy[2], a, a, (g.d, g.ty))
            b = self.half(g.ty, 1)
            comm.recv(self.sy[1], b, (g.d, g.ty))
            comm.send(self.sx[2], b, b, (g.d, g.tx))

    def wait(self, i):
        g, comm = self.g, self.comm
        if i == 0:
            return
        if not g.square:
            comm.recv(self.s[i - 1], self.buf.at[g.rows(g.arrive[i])], (g.d, g.arrive[i]))
        elif i == 1:
            comm.recv(self.sx[1], self.half(g.tx, 1), (g.d, g.tx))
        elif i == 2:
            comm.recv(self.sy[0], self.half(g.ty, 0), (g.d, g.ty))
        else:
            comm.recv(self.sx[2], self.half(g.td, 1), (g.d, g.tx))
            comm.recv(self.sy[2], self.half(g.td, 0), (g.d, g.ty))


def scatter_scratch(g):
    h = g.R // 2
    if g.square:
        return [pltpu.VMEM((3, 2, h, g.D), BF), pltpu.VMEM((2, h, g.D), BF), pltpu.VMEM((2, h, g.D), BF), pltpu.VMEM((2, 2, h, g.D), BF)]
    return [pltpu.VMEM((g.n_t - 1, 2, h, g.D), BF), pltpu.VMEM((1, 8, 128), BF), pltpu.VMEM((1, 8, 128), BF), pltpu.VMEM((g.n_t - 1, 2, h, g.D), BF)]


class Scatter:
    def __init__(self, geo, comm, bufs):
        self.g, self.comm = geo, comm
        self.part, self.into, self.out, self.fin = bufs
        g = geo
        if g.square:
            self.sx, self.sy = comm.slots(3), comm.slots(3)
        else:
            self.s = comm.slots(g.n_t - 1)

    def give(self, i, value):
        g, comm = self.g, self.comm
        h = g.R // 2
        for j in range(2):
            self.part[i, j] = value[j * h : (j + 1) * h].astype(BF)
        if not g.square:
            comm.send(self.s[i], self.part.at[i], self.fin.at[i], (g.d, g.leave[i]))
        elif i == 0:
            comm.send(self.sx[0], self.part.at[0, 0], self.into.at[0], (g.d, g.tx))
            comm.send(self.sy[0], self.part.at[0, 1], self.into.at[1], (g.d, g.ty))
        elif i == 1:
            comm.send(self.sx[1], self.part.at[1, 0], self.fin.at[0, 0], (g.d, g.tx))
        else:
            comm.send(self.sy[1], self.part.at[2, 1], self.fin.at[1, 1], (g.d, g.ty))

    def relay(self):
        g, comm = self.g, self.comm
        if not g.square:
            return
        comm.recv(self.sx[0], self.into.at[0], (g.d, g.tx))
        self.out[0] = (self.into[0].astype(F32) + self.part[2, 0].astype(F32)).astype(BF)
        comm.send(self.sy[2], self.out.at[0], self.fin.at[1, 0], (g.d, g.ty))
        comm.recv(self.sy[0], self.into.at[1], (g.d, g.ty))
        self.out[1] = (self.into[1].astype(F32) + self.part[1, 1].astype(F32)).astype(BF)
        comm.send(self.sx[2], self.out.at[1], self.fin.at[0, 1], (g.d, g.tx))

    def total(self, own):
        g, comm = self.g, self.comm
        h = g.R // 2
        if g.square:
            comm.recv(self.sx[1], self.fin.at[0, 0], (g.d, g.tx))
            comm.recv(self.sy[1], self.fin.at[1, 1], (g.d, g.ty))
            comm.recv(self.sx[2], self.fin.at[0, 1], (g.d, g.tx))
            comm.recv(self.sy[2], self.fin.at[1, 0], (g.d, g.ty))
            count = 2
        else:
            count = g.n_t - 1
            for k in range(count):
                comm.recv(self.s[k], self.fin.at[k], (g.d, g.arrive[k + 1]))
        halves = []
        for j in range(2):
            v = own[j * h : (j + 1) * h]
            for k in range(count):
                v = v + self.fin[k, j].astype(F32)
            halves.append(v)
        return jnp.concatenate(halves, axis=0)


class WeightGather:
    def __init__(self, geo, comm, buf):
        self.g, self.comm, self.buf = geo, comm, buf
        g = geo
        self.sz, self.sc = comm.slots(g.C - 1), comm.slots(g.C)
        own = self.at(g.d)
        for k in range(1, g.C):
            comm.send(self.sz[k - 1], own, own, (g.zto(k), g.t))
        comm.send(self.sc[0], own, own, (g.sib, g.t))

    def at(self, d):
        return self.buf.at[:, self.g.wrows(d)]

    def wait(self):
        g, comm = self.g, self.comm
        for k in range(1, g.C):
            block = self.at(g.zfrom(k))
            comm.recv(self.sz[k - 1], block, (g.zfrom(k), g.t))
            comm.send(self.sc[k], block, block, (g.sib, g.t))
        for k in range(g.C):
            other = g.zfrom(k) + 1 - 2 * g.core
            comm.recv(self.sc[k], self.at(other), (g.sib, g.t))


def rotated(v, cosine, sine):
    n = v.shape[1]
    lower = lax.broadcasted_iota(jnp.int32, v.shape, 1) % HD < HD // 2
    swapped = jnp.where(lower, pltpu.roll(v, n - HD // 2, 1), pltpu.roll(v, HD // 2, 1))
    return v * cosine + swapped * sine


def head_lanes(v, h):
    lane = lax.broadcasted_iota(jnp.int32, v.shape, 1)
    keep = (lane >= h * HD) & (lane < (h + 1) * HD)
    return jnp.where(keep, v, jnp.zeros_like(v))


def bias_of(qinfo, kinfo, first, size, rows):
    shape = (size, rows)
    doc_q, pic_q = qinfo[0:1, :], qinfo[1:2, :]
    key_doc, pic_k, doc_k = kinfo[:, 0:1], kinfo[:, 1:2], kinfo[:, 2:3]
    key_pos = lax.broadcasted_iota(jnp.int32, shape, 0)
    query_pos = lax.broadcasted_iota(jnp.int32, shape, 1) + first
    before = key_pos <= query_pos
    open_ = (doc_q == key_doc) & (before | (pic_q == pic_k))
    ok = open_ | (key_pos == query_pos)
    return jnp.where(ok, 0.0, MASKED).astype(F32)


def k1_body(g, x, wq, wk, wv, wo, wg, wu, wd, cosine, sine, qinfo, kinfo,
            middle, rows, q, kk, v, mixed, probs, rinv, wa, wm, count,
            cnt, bias, vt, part, into, out, fin, ts, tr, zs, zr):
    g.place()
    R, S, c, H = g.R, g.S, g.c, g.H
    tc, zc = Comm(ts, tr, g), Comm(zs, zr, g)
    mine = g.wrows(g.d)
    wa[0, mine] = wq[...]
    wa[1, mine] = wk[...]
    wa[2, mine] = wv[...]
    wa[3, mine] = turned(wo[...])
    one, _ = normed(x[...])
    rows[g.rows(g.t)] = one.astype(BF)
    g.greet()
    ag = Gather(g, tc, rows)
    za = WeightGather(g, zc, wa)
    wm[0, mine] = wg[...]
    wm[1, mine] = wu[...]
    wm[2, mine] = turned(wd[...])
    zm = WeightGather(g, zc, wm)
    sc, sz = zc.slots(1)[0], zc.slots(g.C - 1)
    valid = jnp.sum(qinfo[2:3, :].astype(F32), axis=1, keepdims=True)
    cnt[0] = jnp.broadcast_to(valid, (8, 128))
    zc.send(sc, cnt.at[0], cnt.at[1], (g.sib, g.t))
    zc.recv(sc, cnt.at[1], (g.sib, g.t))
    cnt[2] = cnt[0] + cnt[1]
    for k in range(1, g.C):
        zc.send(sz[k - 1], cnt.at[2], cnt.at[2 + k], (g.zto(k), g.t))
    ag.relay()
    za.wait()
    for i in range(g.n_t):
        ag.wait(i)
        blk = g.rows(g.arrive[i])
        row = rows[blk]
        cos_b, sin_b = cosine[blk], sine[blk]
        q[blk] = (rotated(dot(row, wa[0]), cos_b, sin_b) * HD**-0.5).astype(BF)
        kk[blk] = rotated(dot(row, wa[1]), cos_b, sin_b).astype(BF)
        v[blk] = dot(row, wa[2]).astype(BF)
    vt[...] = turned(v[...])
    sca = Scatter(g, tc, (part, into, out, fin))
    for i, blk in enumerate(g.leave):
        bias[...] = bias_of(qinfo[:, g.rows(blk)], kinfo[...], blk * R, S, R)
        q_blk = q[g.rows(blk)]
        outs = []
        for h in range(H):
            s = dot(kk[...], head_lanes(q_blk, h), NT) + bias[...]
            e = jnp.exp(s - jnp.max(s, axis=0, keepdims=True))
            inv = 1.0 / jnp.sum(e, axis=0, keepdims=True)
            low = e.astype(BF)
            probs[blk, :, h * R : (h + 1) * R] = low
            rinv[blk, h : h + 1, :] = inv
            outs.append(dot(vt[h * HD : (h + 1) * HD, :], low) * inv)
        mix = jnp.concatenate(outs, axis=0).T.astype(BF)
        mixed[g.rows(blk)] = mix
        partial = dot(mix, wa[3], NT)
        if i < g.n_t - 1:
            sca.give(i, partial)
        else:
            middle[...] = x[...] + partial
    sca.relay()
    zm.wait()
    middle[...] = sca.total(middle[...])
    total = cnt[2]
    for k in range(1, g.C):
        zc.recv(sz[k - 1], cnt.at[2 + k], (g.zfrom(k), g.t))
        total = total + cnt[2 + k]
    count[...] = total
    tc.finish()
    zc.finish()


def vmem(*shape_dtype):
    return jax.ShapeDtypeStruct(*shape_dtype)


def call(body, g, name, outs, scratch, cid, args, sems=(24, 24)):
    whole = pl.BlockSpec(memory_space=pltpu.VMEM)
    return pl.pallas_call(
        functools.partial(body, g),
        name=name,
        out_shape=outs,
        in_specs=[whole] * len(args),
        out_specs=[whole] * len(outs),
        scratch_shapes=list(scratch) + [
            pltpu.SemaphoreType.DMA((sems[0],)), pltpu.SemaphoreType.DMA((sems[0],)),
            pltpu.SemaphoreType.DMA((sems[1],)), pltpu.SemaphoreType.DMA((sems[1],)),
        ],
        compiler_params=pltpu.CompilerParams(
            collective_id=cid, has_side_effects=True, vmem_limit_bytes=60 * 2**20
        ),
    )(*args)


def rotary(length, cols):
    half = HD // 2
    frequency = 10000.0 ** (-2.0 * np.arange(half) / HD)
    angle = np.arange(length)[:, None] * frequency[None, :]
    cosine = np.concatenate([np.cos(angle)] * 2, axis=1)
    sine = np.concatenate([-np.sin(angle), np.sin(angle)], axis=1)
    reps = cols // HD
    return (jnp.asarray(np.tile(cosine, (1, reps)), F32), jnp.asarray(np.tile(sine, (1, reps)), F32))


def mask_info(documents, picture_starts, valid_mask):
    length = documents.shape[1]
    at = jnp.arange(length, dtype=jnp.int32)
    starts = picture_starts[0]
    pic = jnp.zeros((length,), jnp.int32)
    for p in range(starts.shape[0]):
        pic = jnp.where((at >= starts[p]) & (at < starts[p] + PIECE), p + 1, pic)
    doc, valid = documents[0], valid_mask[0]
    zero = jnp.zeros_like(doc)
    qinfo = jnp.stack([doc, pic, valid, zero, zero, zero, zero, zero])
    kinfo = jnp.stack([jnp.where(valid == 1, doc, -1), jnp.where(pic > 0, pic, -1), doc], axis=1)
    return qinfo, kinfo


def forward_attention(g, inputs, qinfo, kinfo, tables, weights):
    S, R, D, c, f = g.S, g.R, g.D, g.c, g.f
    sds = jax.ShapeDtypeStruct
    outs = [sds((R, D), F32), sds((S, D), BF), sds((S, c), BF), sds((S, c), BF), sds((S, c), BF), sds((S, c), BF),
            sds((g.n_t, S, g.H * R), BF), sds((g.n_t, 8, R), F32), sds((4, D, c), BF), sds((3, D, f), BF), sds((8, 128), F32)]
    scratch = [pltpu.VMEM((g.C + 2, 8, 128), F32), pltpu.VMEM((S, R), F32), pltpu.VMEM((c, S), BF)] + scatter_scratch(g)
    return call(k1_body, g, "attention_forward", outs, scratch, 1, (inputs, *weights, *tables, qinfo, kinfo))


def gather_rows(block):
    return lax.all_gather(block, "tensor", axis=0, tiled=True)


def scatter_rows(partial_value):
    return lax.psum_scatter(partial_value.astype(BF), "tensor", scatter_dimension=0, tiled=True).astype(F32)


def rotated_back(v, cosine, sine):
    n = v.shape[1]
    lower = lax.broadcasted_iota(jnp.int32, v.shape, 1) % HD < HD // 2
    swapped = jnp.where(lower, jnp.roll(v, -(HD // 2), 1), jnp.roll(v, HD // 2, 1))
    return v * cosine - swapped * sine


def per_device(mesh_shape, inputs, teacher, valid_mask, documents, picture_starts,
               w_query, w_key, w_value, w_out, w_gate, w_up, w_down):
    n_dp, n_t = mesh_shape
    R, D = inputs.shape
    c, f = w_query.shape[1], w_gate.shape[1]
    g = Geo(n_dp, n_t, R, D, c, f)
    length = valid_mask.shape[1]
    tables = rotary(length, c)
    qinfo, kinfo = mask_info(documents, picture_starts, valid_mask)
    weights = (w_query, w_key, w_value, w_out, w_gate, w_up, w_down)
    middle, rows_one, q, kk, v, mixed, probs, rinv, wa, wm, count = forward_attention(g, inputs, qinfo, kinfo, tables, weights)
    tensor_rank = lax.axis_index("tensor")
    row_valid = lax.dynamic_slice_in_dim(valid_mask.reshape(-1), tensor_rank * R, R, 0).astype(F32)[:, None]
    valid_total = count[0, 0]
    one, inv_one = normed(inputs)
    two, inv_two = normed(middle)
    rows_two = gather_rows(two.astype(BF))
    gate_pre, up_proj = dot(rows_two, wm[0]), dot(rows_two, wm[1])
    sg = jax.nn.sigmoid(gate_pre)
    hidden = (gate_pre * sg * up_proj).astype(BF)
    output = middle + scatter_rows(dot(hidden, wm[2], NT))
    deviation = output - teacher
    error = lax.psum(jnp.sum(row_valid * deviation * deviation), ("dp", "tensor"))
    loss_value = error / (D * valid_total)
    cotangent = row_valid * deviation * (length * n_dp / valid_total)
    gm = gather_rows(cotangent.astype(BF))
    down_term = jnp.einsum("gd,gf->df", gm, hidden, preferred_element_type=F32)
    gh = dot(gm, wm[2])
    ggl = (gh * up_proj * sg * (1.0 + gate_pre * (1.0 - sg))).astype(BF)
    gul = (gh * gate_pre * sg).astype(BF)
    gate_term = jnp.einsum("gd,gf->df", rows_two, ggl, preferred_element_type=F32)
    up_term = jnp.einsum("gd,gf->df", rows_two, gul, preferred_element_type=F32)
    gr2 = dot(ggl, wm[0], NT) + dot(gul, wm[1], NT)
    grad_middle = cotangent + normed_back(two, inv_two, scatter_rows(gr2))
    ga = gather_rows(grad_middle.astype(BF))
    out_term = jnp.einsum("gd,gc->dc", ga, mixed, preferred_element_type=F32)
    gmix = dot(ga, wa[3]).astype(BF)
    H, S = g.H, g.S
    pt = (probs.astype(F32).reshape(n_t, S, H, R) * rinv[:, None, :H]).transpose(2, 0, 3, 1).reshape(H, S, S)
    gh_ = gmix.reshape(S, H, HD)
    dp_ = jnp.einsum("qhd,khd->hqk", gh_, v.reshape(S, H, HD), preferred_element_type=F32)
    ds = (pt * (dp_ - jnp.sum(pt * dp_, axis=2, keepdims=True))).astype(BF)
    dq = jnp.einsum("hqk,khd->qhd", ds, kk.reshape(S, H, HD), preferred_element_type=F32).reshape(S, c) * HD**-0.5
    dk = jnp.einsum("hqk,qhd->khd", ds, q.reshape(S, H, HD), preferred_element_type=F32).reshape(S, c)
    dv = jnp.einsum("hqk,qhd->khd", pt.astype(BF), gh_, preferred_element_type=F32).reshape(S, c)
    dq = rotated_back(dq, *tables).astype(BF)
    dk = rotated_back(dk, *tables).astype(BF)
    dv = dv.astype(BF)
    terms = [jnp.einsum("gd,gc->dc", rows_one, t_, preferred_element_type=F32) for t_ in (dq, dk, dv)] + [out_term, gate_term, up_term, down_term]
    gr1 = dot(dq, wa[0], NT) + dot(dk, wa[1], NT) + dot(dv, wa[2], NT)
    grads = [lax.psum_scatter(t_.astype(BF), "dp", scatter_dimension=0, tiled=True).astype(F32) for t_ in terms]
    grad_inputs = grad_middle + normed_back(one, inv_one, scatter_rows(gr1))
    gq, gk, gv, go, gg, gu, gd = grads
    return (output, loss_value, grad_inputs, gq, gk, gv, go.T, gg, gu, gd.T)


def solution(mesh):
    rows, pair = P(("dp", "tensor"), None), P("dp", None)
    cut, across = P("dp", "tensor"), P("tensor", "dp")
    return jax.shard_map(
        functools.partial(per_device, (mesh.shape["dp"], mesh.shape["tensor"])),
        mesh=mesh,
        in_specs=(rows, rows, pair, pair, pair, cut, cut, cut, across, cut, cut, across),
        out_specs=(rows, P(), rows, cut, cut, cut, across, cut, cut, across),
        check_vma=False,
    )
```

time: 807 us -> 622 us (0.77)
  waiting for transfers between devices: 466 us -> 232 us
  Pallas kernels: 0 us -> 90.2 us
  blocking collectives: 102 us -> 40.1 us
  local copies, waits for them, and re-layouts: 50.6 us -> 95 us
  matrix products: 98.1 us -> 87 us
  loops' own time: 11 us -> 0 us
    reduce_scatter x7, waiting for transfers between devices: 297 us -> 158 us  [the longest x3 103 us: scatter_rows(): lax.psum_scatter(partial_value.astype(BF), 'tensor', scatter_dimension=0,...]
    pallas_call x0 -> x1, Pallas kernels: none -> 90.2 us  [call(): pl.pallas_call(functools.partial(body, g), name=name, out_shape=outs, in_...]
    all_gather x4 -> x0, blocking collectives: 62.5 us -> none  [the longest x1 16.6 us: per_device(): lax.all_gather(w_query, 'dp', axis=0, tiled=True)]
    all_gather x3 -> x0, waiting for transfers between devices: 42.5 us -> none  [the longest x1 22.5 us: per_device(): lax.all_gather(w_up, 'dp', axis=0, tiled=True)]
    unnamed x22 -> x16, waiting for transfers between devices: 38.2 us -> 0.24 us
    reshape x0 -> x3, local copies, waits for them, and re-layouts: none -> 37.5 us  [the longest x1 20.7 us: per_device(): (probs.astype(F32).reshape(n_t, S, H, R) * rinv[:, None, :H]).transpose(2...]
    transpose x0 -> x1, local copies, waits for them, and re-layouts: none -> 23.2 us  [per_device(): (probs.astype(F32).reshape(n_t, S, H, R) * rinv[:, None, :H]).transpose(2...]
    dynamic_update_slice x8 -> x0, local copies, waits for them, and re-layouts: 22 us -> none  [the longest x4 21.7 us: attend_backward(): lax.scan(one_block, (zero_rows, zero_rows), (jnp.arange(block_total, dtyp...]
  transfers between devices with their start and end apart: 18 -> 13, of which waited for: 14 -> 7; matrix products, arithmetic and copies ran while one was open for 16% -> 26% of each run, Pallas kernels for 0% -> 0%
where the time goes in v1:
time: 622 us; the launch traced here: 611 us
  waiting for transfers between devices  232 us (37%)
  local copies, waits for them, and re-layouts  95 us (15%)
  Pallas kernels  90.2 us (15%)
  matrix products  87 us (14%)
  other arithmetic  46.1 us (7%)
  blocking collectives  40.1 us (6%)
  between operations  19.3 us (3%)
    reduce_scatter x3, waiting for transfers between devices, scatter_rows(): lax.psum_scatter(partial_value.astype(BF), 'tensor', scatter_dimension=0,...  103 us
    pallas_call x1, Pallas kernels, call(): pl.pallas_call(functools.partial(body, g), name=name, out_shape=outs, in_...  90.2 us
    all_gather x3, waiting for transfers between devices, gather_rows(): return lax.all_gather(block, 'tensor', axis=0, tiled=True)  73.4 us
    reduce_scatter x4, waiting for transfers between devices, per_device(): lax.psum_scatter(t_.astype(BF), 'dp', scatter_dimension=0, tiled=True)  55.4 us
    psum x1, blocking collectives, per_device(): lax.psum(jnp.sum(row_valid * deviation * deviation), ('dp', 'tensor'))  40.1 us
    dot_general x10, matrix products, dot(): return lax.dot_general(a, b, dims, preferred_element_type=F32)  35.8 us
    unnamed x81, local copies, waits for them, and re-layouts  24.6 us
    transpose x1, local copies, waits for them, and re-layouts, per_device(): (probs.astype(F32).reshape(n_t, S, H, R) * rinv[:, None, :H]).transpose(2...  23.2 us
  transfers between devices with their start and end apart: 13, of which 7 were waited for; matrix products, arithmetic and copies ran while one was open for 26% of the time, Pallas kernels for 0%

profile of v1, /device:TPU:0, one launch (start us, length us, event | category | flops | bytes accessed | tf_op | source)
XLA Modules:
  0.0 611.2 jit_solution(16278976575790777135)
XLA Ops:
  19.7 90.2 %attention_forward.1 = (f32[256,1024]{1,0:T(8,128)}, bf16[1024,1024]{1,0:T(8,128)(2,1)}, bf16[1024,256]{1,0:T(8,128)(2,1)}, bf16[1024,256]{1,0:T(8,128)(2,1)}, b...) custom-call(f32[256,1024]{1,0:T(8,128)} %x.1, ...), custom_call_target="tpu_custom_call" | custom-call | tf_op jit(solution)/shard_map/attention_forward/pallas_call | solution.py:369
  113.9 38.0 %all-gather.4.cloned.1.call-done = bf16[1024,1024]{1,0:T(8,128)(2,1)} async-done(((bf16[256,1024]{1,0:T(8,128)(2,1)}), bf16[1024,1024]{1,0:T(8,128)(2,1)}) %all-gather.4.cloned.1.call-update) | async-done | bytes 2097168 | tf_op jit(solution)/shard_map/all_gather | solution.py:419
  152.0 3.9 fusion.10
  155.9 6.0 multiply_convert_fusion.3
  163.0 4.6 convolution_convert_fusion
  170.3 32.7 %reduce-scatter.17.cloned.1.call-done = bf16[256,1024]{1,0:T(8,128)(2,1)} async-done(((bf16[1024,1024]{1,0:T(8,128)(2,1)}), bf16[256,1024]{1,0:T(8,128)(2,1)}) %reduce-scatter.17.cloned.1.call-update) | async-done | bytes 524304 | tf_op jit(solution)/shard_map/reduce_scatter | solution.py:423
  205.6 35.3 %all-gather.6.cloned.1.call-done = bf16[1024,1024]{1,0:T(8,128)(2,1)} async-done(((bf16[256,1024]{1,0:T(8,128)(2,1)}), bf16[1024,1024]{1,0:T(8,128)(2,1)}) %all-gather.6.cloned.1.call-update) | async-done | bytes 2097168 | tf_op jit(solution)/shard_map/all_gather | solution.py:419
  240.9 6.4 %multiply_convert_fusion.1 = (bf16[1024,704]{0,1:T(8,128)(2,1)S(1)}, bf16[1024,704]{0,1:T(8,128)(2,1)S(1)}) fusion(f32[1024,704]{0,1:T(8,128)} %copy-done.28, f32[1024,704]{0,1:T(8,128)} %get-tuple-element.86, bf16[1024,1024]{1,0:T(8,128)(2,1)} %all-gather.6.cloned.1.call-done, bf16[3,1024,704]{2,1,0:T(8,128)(2,1)} %get-tuple-element.22), kind=kOutput, calls=%fused_computation.7 | convolution fusion | flops 1485766656 | bytes 12320768 | tf_op jit(solution)/shard_map/dot_general | solution.py:23
  247.3 4.3 fusion.8
  251.7 4.6 add_convert_fusion.1
  256.3 35.3 %reduce-scatter.19.cloned.1.call-done = bf16[256,1024]{1,0:T(8,128)(2,1)} async-done(((bf16[1024,1024]{1,0:T(8,128)(2,1)}), bf16[256,1024]{1,0:T(8,128)(2,1)}) %reduce-scatter.19.cloned.1.call-update) | async-done | bytes 524304 | tf_op jit(solution)/shard_map/reduce_scatter | solution.py:423
  309.1 16.5 %reshape.219 = f32[4,1024,4,256]{3,2,1,0:T(4,128)} reshape(bf16[4,1024,1024]{2,1,0:T(8,128)(2,1)} %get-tuple-element.25) | data formatting | bytes 25165824 | tf_op jit(solution)/shard_map/reshape | solution.py:471
  325.6 8.9 %multiply_bitcast_fusion = f32[4,4,256,1024]{2,0,3,1:T(4,128)S(1)} fusion(f32[4,1024,4,256]{3,2,1,0:T(4,128)} %reshape.219, f32[4,4,256]{2,1,0:T(4,128)S(1)} %slice.74), kind=kLoop, calls=%fused_computation.2 | loop fusion | flops 4194304 | bytes 33570816 | tf_op jit(solution)/shard_map/transpose | solution.py:471
  334.5 23.2 %copy.63 = f32[4,4,256,1024]{2,1,3,0:T(4,128)} copy(f32[4,4,256,1024]{2,0,3,1:T(4,128)S(1)} %multiply_bitcast_fusion) | data formatting | bytes 33554432 | tf_op jit(solution)/shard_map/transpose | solution.py:471
  357.7 20.7 %reshape.213 = f32[4,1024,1024]{1,2,0:T(8,128)} reshape(f32[4,4,256,1024]{2,1,3,0:T(4,128)} %copy.63) | data formatting | bytes 33554432 | tf_op jit(solution)/shard_map/reshape | solution.py:471
  378.5 4.8 convolution_convert_fusion.1
  388.7 14.9 %multiply_reduce_fusion = (f32[4,1024]{1,0:T(4,128)S(1)}, f32[4,1024,1024]{1,2,0:T(8,128)}) fusion(f32[4,1024,1024]{1,2,0:T(8,128)} %reshape.213, bf16[1024,4,64]{0,2,1:T(8,128)(2,1)S(1)} %bitcast.99, bf16[1024,4,64]{0,2,1:T(8,128)(2,1)S(1)} %bitcast.101), kind=kOutput, calls=%fused_computation.1 | convolution fusion | flops 545255424 | bytes 34619392 | tf_op jit(solution)/shard_map/qhd,khd->hqk/dot_general | solution.py:473
  405.4 7.9 %multiply_convert_fusion = bf16[4,1024,1024]{1,2,0:T(8,128)(2,1)S(1)} fusion(f32[4,1024,1024]{1,2,0:T(8,128)S(1)} %bitcast.96, f32[4,1024,1024]{1,2,0:T(8,128)} %get-tuple-element.88, f32[4,1024]{1,0:T(4,128)S(1)} %get-tuple-element.87), kind=kLoop, calls=%fused_computation | loop fusion | flops 12582912 | bytes 41959424 | tf_op jit(solution)/shard_map/convert_element_type | solution.py:474
  417.0 6.3 %fusion.56 = f32[4,64,1024]{2,1,0:T(8,128)S(1)} fusion(bf16[1024,4,64]{0,2,1:T(8,128)(2,1)} %bitcast.105, bf16[4,1024,1024]{1,2,0:T(8,128)(2,1)} %copy-done), kind=kOutput, calls=%fused_computation.107 | convolution fusion | flops 536870912 | bytes 9961472 | tf_op jit(solution)/shard_map/hqk,qhd->khd/dot_general | solution.py:476
  428.4 8.9 %fusion.18 = bf16[4,64,1024]{2,1,0:T(8,128)(2,1)S(1)} fusion(bf16[1024,4,64]{0,2,1:T(8,128)(2,1)} %bitcast.100, f32[4,1024,1024]{1,2,0:T(8,128)} %reshape.213), kind=kOutput, calls=%fused_computation.40 | convolution fusion | flops 541327360 | bytes 17825792 | tf_op jit(solution)/shard_map/hqk,qhd->khd/dot_general | solution.py:477
  462.1 40.1 %psum.7 = f32[]{:T(128)} all-reduce(f32[]{:T(128)} %get-tuple-element.74), channel_id=1, replica_groups=mesh['dp'=8,'tensor'=4] {'dp','tensor'}, use_global_device_ids=true, to_apply=%region_4.5 | all-reduce | flops 1 | bytes 8 | tf_op jit(solution)/shard_map/psum | solution.py:455
  506.0 25.6 %reduce-scatter.25.cloned.1.call-done = bf16[128,256]{1,0:T(8,128)(2,1)} async-done(((bf16[1024,256]{1,0:T(8,128)(2,1)}), bf16[128,256]{1,0:T(8,128)(2,1)}) %reduce-scatter.25.cloned.1.call-update) | async-done | bytes 65552 | tf_op jit(solution)/shard_map/reduce_scatter | solution.py:483
  533.0 29.9 %reduce-scatter.23.cloned.1.call-done = bf16[128,256]{1,0:T(8,128)(2,1)} async-done(((bf16[1024,256]{1,0:T(8,128)(2,1)}), bf16[128,256]{1,0:T(8,128)(2,1)}) %reduce-scatter.23.cloned.1.call-update) | async-done | bytes 65552 | tf_op jit(solution)/shard_map/reduce_scatter | solution.py:483
  564.4 34.9 %reduce-scatter.21.cloned.1.call-done = bf16[256,1024]{1,0:T(8,128)(2,1)} async-done(((bf16[1024,1024]{1,0:T(8,128)(2,1)}), bf16[256,1024]{1,0:T(8,128)(2,1)}) %reduce-scatter.21.cloned.1.call-update) | async-done | bytes 524304 | tf_op jit(solution)/shard_map/reduce_scatter | solution.py:423
  (173 shorter events, 88.1 us)
Async XLA Ops:
  7.2 144.8 %all-gather.4.cloned.1.call-start = ((), (), s32[]{:S(2)}) async-start(), calls=%async_computation.10 | async-start | bytes 2621440 | tf_op jit(solution)/shard_map/all_gather | solution.py:419
  113.9 89.1 %reduce-scatter.17.cloned.1.call-start = ((), (), s32[]{:S(2)}) async-start(), calls=%async_computation.11 | async-start | bytes 2621440 | tf_op jit(solution)/shard_map/reduce_scatter | solution.py:423
  155.9 6.0 copy-start.28
  167.6 35.4 %copy-start.5 = (f32[256,1024]{1,0:T(8,128)S(1)}, f32[256,1024]{1,0:T(8,128)}, u32[]{:S(2)}) copy-start(f32[256,1024]{1,0:T(8,128)} %param.15) | copy-start | bytes 3145732
  167.6 73.3 %all-gather.6.cloned.1.call-start = ((), (), s32[]{:S(2)}) async-start(), calls=%async_computation.12 | async-start | bytes 2621440 | tf_op jit(solution)/shard_map/all_gather | solution.py:419
  205.1 88.0 %copy-start.6 = (f32[256,1024]{1,0:T(8,128)}, f32[256,1024]{1,0:T(8,128)S(1)}, u32[]{:S(2)}) copy-start(f32[256,1024]{1,0:T(8,128)S(1)} %get-tuple-element.69) | copy-start | bytes 3145732
  205.1 86.6 %reduce-scatter.19.cloned.1.call-start = ((), (), s32[]{:S(2)}) async-start(), calls=%async_computation.13 | async-start | bytes 2621440 | tf_op jit(solution)/shard_map/reduce_scatter | solution.py:423
  247.3 4.4 copy-start.29
  256.3 129.9 %all-gather.8.cloned.1.call-start = ((), (), s32[]{:S(2)}) async-start(), calls=%async_computation.14 | async-start | bytes 2621440 | tf_op jit(solution)/shard_map/all_gather | solution.py:419
  296.5 160.0 %reduce-scatter.33.cloned.1.call-start = ((), (), s32[]{:S(2)}) async-start(), calls=%async_computation.21 | async-start | bytes 1769472
  301.9 156.4 %reduce-scatter.31.cloned.1.call-start = ((), (), s32[]{:S(2)}) async-start(), calls=%async_computation.20 | async-start | bytes 1769472
  307.1 153.1 %reduce-scatter.35.cloned.1.call-start = ((), (), s32[]{:S(2)}) async-start(), calls=%async_computation.22 | async-start | bytes 1769472
  385.9 117.0 %reduce-scatter.29.cloned.1.call-start = ((), (), s32[]{:S(2)}) async-start(), calls=%async_computation.19 | async-start | bytes 589824 | tf_op jit(solution)/shard_map/reduce_scatter | solution.py:483
  388.6 14.9 %copy-start.9 = (bf16[1024,256]{0,1:T(8,128)(2,1)}, bf16[1024,256]{0,1:T(8,128)(2,1)S(1)}, u32[]{:S(2)}) copy-start(bf16[1024,256]{0,1:T(8,128)(2,1)S(1)} %convolution_convert_fusion.8) | copy-start | bytes 1572868
  388.6 14.9 %slice-start = ((s8[16777216]{0:T(1024)(128)(4,1)}), s8[4194304]{0:T(1024)(128)(4,1)S(1)}, s32[]{:S(2)}) async-start(s8[16777216]{0:T(1024)(128)(4,1)} %bitcast.95), calls=%async_computation.23 | async-start | bytes 8388608
  388.7 14.9 %slice-start.1 = ((s8[16777216]{0:T(1024)(128)(4,1)}), s8[4194304]{0:T(1024)(128)(4,1)S(1)}, s32[]{:S(2)}) async-start(s8[16777216]{0:T(1024)(128)(4,1)} %bitcast.95), calls=%async_computation.24 | async-start | bytes 8388608
  388.7 14.9 %slice-start.2 = ((s8[16777216]{0:T(1024)(128)(4,1)}), s8[4194304]{0:T(1024)(128)(4,1)S(1)}, s32[]{:S(2)}) async-start(s8[16777216]{0:T(1024)(128)(4,1)} %bitcast.95), calls=%async_computation.25 | async-start | bytes 8388608
  388.7 16.8 %slice-start.3 = ((s8[16777216]{0:T(1024)(128)(4,1)}), s8[4194304]{0:T(1024)(128)(4,1)S(1)}, s32[]{:S(2)}) async-start(s8[16777216]{0:T(1024)(128)(4,1)} %bitcast.95), calls=%async_computation.26 | async-start | bytes 8388608
  428.3 76.2 %reduce-scatter.27.cloned.1.call-start = ((), (), s32[]{:S(2)}) async-start(), calls=%async_computation.18 | async-start | bytes 589824 | tf_op jit(solution)/shard_map/reduce_scatter | solution.py:483
  428.4 9.7 %copy-start.22 = (bf16[1024,1024]{1,0:T(8,128)(2,1)S(1)}, bf16[1024,1024]{1,0:T(8,128)(2,1)}, u32[]{:S(2)}) copy-start(bf16[1024,1024]{1,0:T(8,128)(2,1)} %get-tuple-element.30) | copy-start | bytes 6291460
  439.7 91.9 %reduce-scatter.25.cloned.1.call-start = ((), (), s32[]{:S(2)}) async-start(), calls=%async_computation.17 | async-start | bytes 589824 | tf_op jit(solution)/shard_map/reduce_scatter | solution.py:483
  446.6 116.3 %reduce-scatter.23.cloned.1.call-start = ((), (), s32[]{:S(2)}) async-start(), calls=%async_computation.16 | async-start | bytes 589824 | tf_op jit(solution)/shard_map/reduce_scatter | solution.py:483
  450.0 149.3 %reduce-scatter.21.cloned.1.call-start = ((), (), s32[]{:S(2)}) async-start(), calls=%async_computation.15 | async-start | bytes 2621440 | tf_op jit(solution)/shard_map/reduce_scatter | solution.py:423
  459.4 141.3 %copy-start.8 = (f32[256,1024]{1,0:T(8,128)S(1)}, f32[256,1024]{1,0:T(8,128)}, u32[]{:S(2)}) copy-start(f32[256,1024]{1,0:T(8,128)} %get-tuple-element.67) | copy-start | bytes 3145732
  (25 other events, 49.9 us)
Sparse Core Ops, SparseCore 0:
  114.0 37.9 all-gather.3
  167.7 35.1 reduce-scatter.16
  205.5 35.2 all-gather.5
  256.4 35.2 reduce-scatter.18
  296.6 35.2 all-gather.7
  334.1 34.2 reduce-scatter.32
  370.7 32.2 reduce-scatter.30
  405.3 31.9 reduce-scatter.34
  439.6 28.9 reduce-scatter.28
  470.8 29.2 reduce-scatter.26
  502.3 29.1 reduce-scatter.24
  533.7 29.1 reduce-scatter.22
  565.9 33.3 reduce-scatter.20
